TPU v7x, 32 devices: a whole 2x2x4 slice. The times are simulated.
32 devices in a mesh: ctx: 16 (over z, y, x), fsdp: 2 (over core).
Axes of the slice: x: 2, y: 2, z: 4, core: 2. Of those that a mesh axis runs over, the one named last changes fastest.
Arguments:
- x_in: bfloat16 [4, 1024, 576], P('fsdp', 'ctx')
- w_query: bfloat16 [576, 576], P('fsdp'), may hold values from -0.25 to 0.25
- w_key: bfloat16 [576, 192], P('fsdp'), may hold values from -0.25 to 0.25
- w_value: bfloat16 [576, 192], P('fsdp'), may hold values from -0.25 to 0.25
- w_out: bfloat16 [576, 576], P('fsdp'), may hold values from -6 to 6
- attn_gain: bfloat16 [576], P('fsdp'), may hold values from 0.5 to 1.5
- w_gate: bfloat16 [576, 1536], P('fsdp'), may hold values from -0.25 to 0.25
- w_up: bfloat16 [576, 1536], P('fsdp'), may hold values from -0.25 to 0.25
- w_down: bfloat16 [1536, 576], P('fsdp'), may hold values from -0.15625 to 0.15625
- mlp_gain: bfloat16 [576], P('fsdp'), may hold values from 0.5 to 1.5
- block_of_slot: int32 [32], replicated, may hold values from 0 to 31, as said below
- out_grad: bfloat16 [4, 1024, 576], P('fsdp', 'ctx'), may hold values from -6 to 6
Outputs:
- y_out: bfloat16 [4, 1024, 576], P('fsdp', 'ctx')
- x_grad: bfloat16 [4, 1024, 576], P('fsdp', 'ctx')
- grad_w_query: float32 [576, 576], P('fsdp')
- grad_w_key: float32 [576, 192], P('fsdp')
- grad_w_value: float32 [576, 192], P('fsdp')
- grad_w_out: float32 [576, 576], P('fsdp')
- grad_attn_gain: float32 [576], P('fsdp')
- grad_w_gate: float32 [576, 1536], P('fsdp')
- grad_w_up: float32 [576, 1536], P('fsdp')
- grad_w_down: float32 [1536, 576], P('fsdp')
- grad_mlp_gain: float32 [576], P('fsdp')
Inputs may be any that keep to these rules, and one draw needn't show every extreme that they name: `block_of_slot`: the entries are a permutation of 0 to 31 and entries 2 i and 2 i + 1 sum to 31, so slots 2 i and 2 i + 1 hold a block from the front of the sequence and its mirror from the back.
All inputs are finite; a program needn't handle non-finite values.
Results may differ from a plain program's by a relative error of at most 0.025.
Values may be sent and summed in bfloat16 or wider, within the bound.
A program may use at most 128 MiB of HBM per device.

v0:
```python
import jax
import jax.numpy as jnp
from jax import lax
from jax.sharding import PartitionSpec as P

HEADS = 9
KV_HEADS = 3
HEAD_DIM = 64
epsilon = 1e-05
theta_base = 100000.0
masked_value = -1e30


def shifted(block, axis, distance):
    devices = range(lax.axis_size(axis))
    route = [((i - distance) % len(devices), i) for i in devices]
    return lax.ppermute(block, axis, route)


def make_tables(positions):
    half_dim = HEAD_DIM // 2
    frequency = theta_base ** (-2.0 * jnp.arange(half_dim, dtype=jnp.float32) / HEAD_DIM)
    angles = positions.astype(jnp.float32)[:, None] * frequency[None, :]
    return (jnp.cos(angles), jnp.sin(angles))


def rotate(values, cosine, sine):
    half_dim = values.shape[-1] // 2
    first_half = values[..., :half_dim]
    second_half = values[..., half_dim:]
    cos_rows = cosine[:, None, :]
    sin_rows = sine[:, None, :]
    return jnp.concatenate(
        [
            first_half * cos_rows - second_half * sin_rows,
            second_half * cos_rows + first_half * sin_rows,
        ],
        axis=-1,
    )


def rotate_back(grads, cosine, sine):
    half_dim = grads.shape[-1] // 2
    first_half = grads[..., :half_dim]
    second_half = grads[..., half_dim:]
    cos_rows = cosine[:, None, :]
    sin_rows = sine[:, None, :]
    return jnp.concatenate(
        [
            first_half * cos_rows + second_half * sin_rows,
            second_half * cos_rows - first_half * sin_rows,
        ],
        axis=-1,
    )


def slot_positions(block_of_slot, offset, count_rows, half_len):
    row_ids = offset + jnp.arange(count_rows, dtype=jnp.int32)
    slot_ids = row_ids // half_len
    slot_match = slot_ids[:, None] == jnp.arange(block_of_slot.shape[0], dtype=jnp.int32)[None, :]
    owners = jnp.sum(jnp.where(slot_match, block_of_slot[None, :], 0), axis=1)
    return owners * half_len + row_ids % half_len


def norm_forward(values, gain_vec):
    inverse = lax.rsqrt(jnp.mean(values * values, axis=-1, keepdims=True) + epsilon)
    scaled = values * inverse
    return (scaled * gain_vec, scaled, inverse)


def norm_backward(grad_output, gain_vec, scaled, inverse):
    grad_scaled = grad_output * gain_vec
    grad_input = inverse * (
        grad_scaled - scaled * jnp.mean(grad_scaled * scaled, axis=-1, keepdims=True)
    )
    grad_gain = jnp.sum(grad_output * scaled, axis=0)
    return (grad_input, grad_gain)


def local(
    x_in,
    w_query,
    w_key,
    w_value,
    w_out,
    attn_gain,
    w_gate,
    w_up,
    w_down,
    mlp_gain,
    block_of_slot,
    out_grad,
):
    gathered = (
        lax.all_gather(w_query, "fsdp", axis=0, tiled=True),
        lax.all_gather(w_key, "fsdp", axis=0, tiled=True),
        lax.all_gather(w_value, "fsdp", axis=0, tiled=True),
        lax.all_gather(w_out, "fsdp", axis=0, tiled=True),
        lax.all_gather(attn_gain, "fsdp", axis=0, tiled=True),
        lax.all_gather(w_gate, "fsdp", axis=0, tiled=True),
        lax.all_gather(w_up, "fsdp", axis=0, tiled=True),
        lax.all_gather(w_down, "fsdp", axis=0, tiled=True),
        lax.all_gather(mlp_gain, "fsdp", axis=0, tiled=True),
    )
    (
        full_query,
        full_key,
        full_value,
        full_out,
        gain_attn,
        full_gate,
        full_up,
        full_down,
        gain_mlp,
    ) = gathered
    gain_attn_f = gain_attn.astype(jnp.float32)
    gain_mlp_f = gain_mlp.astype(jnp.float32)
    seq_count, tok_count, model_width = x_in.shape
    group_size = HEADS // KV_HEADS
    half_len = tok_count // 2
    rows_all = seq_count * tok_count
    ctx_count = lax.axis_size("ctx")
    score_scale = HEAD_DIM ** (-0.5)
    my_offset = lax.axis_index("ctx") * tok_count
    query_pos = slot_positions(block_of_slot, my_offset, tok_count, half_len)
    cosine, sine = make_tables(query_pos)
    inputs = x_in.astype(jnp.float32).reshape(rows_all, model_width)
    normed_f, scaled_one, inverse_one = norm_forward(inputs, gain_attn_f)
    normed = normed_f.astype(jnp.bfloat16)
    query_f = jnp.dot(normed, full_query, preferred_element_type=jnp.float32).reshape(
        seq_count, tok_count, HEADS, HEAD_DIM
    )
    queries = (
        rotate(query_f, cosine, sine)
        .astype(jnp.bfloat16)
        .reshape(seq_count, tok_count, KV_HEADS, group_size, HEAD_DIM)
    )
    key_f = jnp.dot(normed, full_key, preferred_element_type=jnp.float32).reshape(
        seq_count, tok_count, KV_HEADS, HEAD_DIM
    )
    key_rows = rotate(key_f, cosine, sine).astype(jnp.bfloat16)
    value_rows = (
        jnp.dot(normed, full_value, preferred_element_type=jnp.float32)
        .astype(jnp.bfloat16)
        .reshape(seq_count, tok_count, KV_HEADS, HEAD_DIM)
    )
    stat_shape = (seq_count, KV_HEADS, group_size, tok_count)
    running_max = jnp.full(stat_shape, masked_value, jnp.float32)
    key_part = lax.all_gather(key_rows, "ctx", axis=1, tiled=True)
    value_part = lax.all_gather(value_rows, "ctx", axis=1, tiled=True)
    key_pos = slot_positions(block_of_slot, jnp.int32(0), key_part.shape[1], half_len)
    visible = query_pos[:, None] >= key_pos[None, :]
    scores = (
        jnp.einsum("sqkgd,snkd->skgqn", queries, key_part, preferred_element_type=jnp.float32)
        * score_scale
    )
    scores = jnp.where(visible, scores, masked_value)
    new_max = jnp.maximum(running_max, jnp.max(scores, axis=-1))
    weights = jnp.where(visible, jnp.exp(scores - new_max[..., None]), 0.0)
    totals = jnp.sum(weights, axis=-1)
    weighted_sum = jnp.einsum(
        "skgqn,snkd->skgqd",
        weights.astype(jnp.bfloat16),
        value_part,
        preferred_element_type=jnp.float32,
    )
    running_max, totals, weighted_sum = (new_max, totals, weighted_sum)
    log_total = running_max + jnp.log(totals)
    attended_f = weighted_sum / totals[..., None]
    attended = (
        attended_f.transpose(0, 3, 1, 2, 4).reshape(rows_all, model_width).astype(jnp.bfloat16)
    )
    hidden_state = inputs + jnp.dot(attended, full_out, preferred_element_type=jnp.float32)
    normed_two_f, scaled_two, inverse_two = norm_forward(hidden_state, gain_mlp_f)
    normed_two = normed_two_f.astype(jnp.bfloat16)
    gate_vals = jnp.dot(normed_two, full_gate, preferred_element_type=jnp.float32)
    up_vals = jnp.dot(normed_two, full_up, preferred_element_type=jnp.float32)
    sigmoid_gate = jax.nn.sigmoid(gate_vals)
    activated = gate_vals * sigmoid_gate
    inner_rows = (activated * up_vals).astype(jnp.bfloat16)
    result = hidden_state + jnp.dot(inner_rows, full_down, preferred_element_type=jnp.float32)
    y_out = result.reshape(seq_count, tok_count, model_width).astype(jnp.bfloat16)
    grad_top = out_grad.reshape(rows_all, model_width)
    grad_residual = grad_top.astype(jnp.float32)
    grad_wdown = jnp.einsum("rf,rd->fd", inner_rows, grad_top, preferred_element_type=jnp.float32)
    grad_inner = jnp.einsum("rd,fd->rf", grad_top, full_down, preferred_element_type=jnp.float32)
    grad_gate = (
        grad_inner * up_vals * sigmoid_gate * (1.0 + gate_vals * (1.0 - sigmoid_gate))
    ).astype(jnp.bfloat16)
    grad_up = (grad_inner * activated).astype(jnp.bfloat16)
    grad_wgate = jnp.einsum("rd,rf->df", normed_two, grad_gate, preferred_element_type=jnp.float32)
    grad_wup = jnp.einsum("rd,rf->df", normed_two, grad_up, preferred_element_type=jnp.float32)
    grad_normed_two = jnp.einsum(
        "rf,df->rd", grad_gate, full_gate, preferred_element_type=jnp.float32
    ) + jnp.einsum("rf,df->rd", grad_up, full_up, preferred_element_type=jnp.float32)
    grad_hidden_norm, grad_gain_mlp = norm_backward(
        grad_normed_two, gain_mlp_f, scaled_two, inverse_two
    )
    grad_hidden = grad_residual + grad_hidden_norm
    grad_branch = grad_hidden.astype(jnp.bfloat16)
    grad_wout = jnp.einsum("ri,rj->ij", attended, grad_branch, preferred_element_type=jnp.float32)
    grad_attended = jnp.einsum(
        "rj,ij->ri", grad_branch, full_out, preferred_element_type=jnp.float32
    ).astype(jnp.bfloat16)
    grad_heads = grad_attended.reshape(
        seq_count, tok_count, KV_HEADS, group_size, HEAD_DIM
    ).transpose(0, 2, 3, 1, 4)
    row_delta = jnp.sum(grad_heads.astype(jnp.float32) * attended_f, axis=-1)

    def block_grads(key_part, value_part, offset):
        key_pos = slot_positions(block_of_slot, offset, key_part.shape[1], half_len)
        visible = query_pos[:, None] >= key_pos[None, :]
        scores = (
            jnp.einsum("sqkgd,snkd->skgqn", queries, key_part, preferred_element_type=jnp.float32)
            * score_scale
        )
        weights = jnp.where(visible, jnp.exp(scores - log_total[..., None]), 0.0)
        grad_value_part = jnp.einsum(
            "skgqn,skgqd->snkd",
            weights.astype(jnp.bfloat16),
            grad_heads,
            preferred_element_type=jnp.float32,
        )
        grad_weights = jnp.einsum(
            "skgqd,snkd->skgqn", grad_heads, value_part, preferred_element_type=jnp.float32
        )
        grad_scores = (weights * (grad_weights - row_delta[..., None])).astype(jnp.bfloat16)
        grad_query_part = jnp.einsum(
            "skgqn,snkd->skgqd", grad_scores, key_part, preferred_element_type=jnp.float32
        )
        grad_key_part = (
            jnp.einsum(
                "skgqn,sqkgd->snkd", grad_scores, queries, preferred_element_type=jnp.float32
            )
            * score_scale
        )
        return (grad_query_part, grad_key_part, grad_value_part)

    grad_query_init = jnp.zeros(stat_shape + (HEAD_DIM,), jnp.float32)
    kv_zero = jnp.zeros(key_rows.shape, jnp.float32)

    def one_hop(hop_index, loop_state):
        key_part, value_part, grad_query, grad_key, grad_value = loop_state
        source = (lax.axis_index("ctx") - hop_index) % ctx_count
        grad_query_part, grad_key_part, grad_value_part = block_grads(
            key_part, value_part, source * tok_count
        )
        key_part, value_part = shifted((key_part, value_part), "ctx", 1)
        grad_key, grad_value = (
            shifted((grad_key + grad_key_part).astype(jnp.bfloat16), "ctx", 1).astype(jnp.float32),
            shifted((grad_value + grad_value_part).astype(jnp.bfloat16), "ctx", 1).astype(
                jnp.float32
            ),
        )
        return (key_part, value_part, grad_query + grad_query_part, grad_key, grad_value)

    loop_state = lax.fori_loop(
        0, ctx_count - 1, one_hop, (key_rows, value_rows, grad_query_init, kv_zero, kv_zero)
    )
    key_part, value_part, grad_query, grad_key, grad_value = loop_state
    source = (lax.axis_index("ctx") + 1) % ctx_count
    grad_query_part, grad_key_part, grad_value_part = block_grads(
        key_part, value_part, source * tok_count
    )
    grad_query = grad_query + grad_query_part
    grad_key, grad_value = (
        shifted((grad_key + grad_key_part).astype(jnp.bfloat16), "ctx", 1).astype(jnp.float32),
        shifted((grad_value + grad_value_part).astype(jnp.bfloat16), "ctx", 1).astype(jnp.float32),
    )
    grad_query_rows = (
        (grad_query * score_scale)
        .transpose(0, 3, 1, 2, 4)
        .reshape(seq_count, tok_count, HEADS, HEAD_DIM)
    )
    grad_query_low = (
        rotate_back(grad_query_rows, cosine, sine)
        .astype(jnp.bfloat16)
        .reshape(rows_all, model_width)
    )
    grad_key_low = (
        rotate_back(grad_key, cosine, sine)
        .astype(jnp.bfloat16)
        .reshape(rows_all, KV_HEADS * HEAD_DIM)
    )
    grad_value_low = grad_value.astype(jnp.bfloat16).reshape(rows_all, KV_HEADS * HEAD_DIM)
    grad_wquery = jnp.einsum(
        "rd,re->de", normed, grad_query_low, preferred_element_type=jnp.float32
    )
    grad_wkey = jnp.einsum("rd,re->de", normed, grad_key_low, preferred_element_type=jnp.float32)
    grad_wvalue = jnp.einsum(
        "rd,re->de", normed, grad_value_low, preferred_element_type=jnp.float32
    )
    grad_normed = jnp.einsum(
        "re,de->rd", grad_query_low, full_query, preferred_element_type=jnp.float32
    )
    grad_normed = grad_normed + jnp.einsum(
        "re,de->rd", grad_key_low, full_key, preferred_element_type=jnp.float32
    )
    grad_normed = grad_normed + jnp.einsum(
        "re,de->rd", grad_value_low, full_value, preferred_element_type=jnp.float32
    )
    grad_input_norm, grad_gain_attn = norm_backward(
        grad_normed, gain_attn_f, scaled_one, inverse_one
    )
    x_grad = (
        (grad_hidden + grad_input_norm)
        .astype(jnp.bfloat16)
        .reshape(seq_count, tok_count, model_width)
    )
    owned_grads = (
        lax.psum_scatter(
            grad_wquery.astype(jnp.bfloat16), "fsdp", scatter_dimension=0, tiled=True
        ).astype(jnp.float32),
        lax.psum_scatter(
            grad_wkey.astype(jnp.bfloat16), "fsdp", scatter_dimension=0, tiled=True
        ).astype(jnp.float32),
        lax.psum_scatter(
            grad_wvalue.astype(jnp.bfloat16), "fsdp", scatter_dimension=0, tiled=True
        ).astype(jnp.float32),
        lax.psum_scatter(
            grad_wout.astype(jnp.bfloat16), "fsdp", scatter_dimension=0, tiled=True
        ).astype(jnp.float32),
        lax.psum_scatter(
            grad_gain_attn.astype(jnp.bfloat16), "fsdp", scatter_dimension=0, tiled=True
        ).astype(jnp.float32),
        lax.psum_scatter(
            grad_wgate.astype(jnp.bfloat16), "fsdp", scatter_dimension=0, tiled=True
        ).astype(jnp.float32),
        lax.psum_scatter(
            grad_wup.astype(jnp.bfloat16), "fsdp", scatter_dimension=0, tiled=True
        ).astype(jnp.float32),
        lax.psum_scatter(
            grad_wdown.astype(jnp.bfloat16), "fsdp", scatter_dimension=0, tiled=True
        ).astype(jnp.float32),
        lax.psum_scatter(
            grad_gain_mlp.astype(jnp.bfloat16), "fsdp", scatter_dimension=0, tiled=True
        ).astype(jnp.float32),
    )
    summed_grads = (
        lax.psum(owned_grads[0].astype(jnp.bfloat16), "ctx").astype(jnp.float32),
        lax.psum(owned_grads[1].astype(jnp.bfloat16), "ctx").astype(jnp.float32),
        lax.psum(owned_grads[2].astype(jnp.bfloat16), "ctx").astype(jnp.float32),
        lax.psum(owned_grads[3].astype(jnp.bfloat16), "ctx").astype(jnp.float32),
        lax.psum(owned_grads[4].astype(jnp.bfloat16), "ctx").astype(jnp.float32),
        lax.psum(owned_grads[5].astype(jnp.bfloat16), "ctx").astype(jnp.float32),
        lax.psum(owned_grads[6].astype(jnp.bfloat16), "ctx").astype(jnp.float32),
        lax.psum(owned_grads[7].astype(jnp.bfloat16), "ctx").astype(jnp.float32),
        lax.psum(owned_grads[8].astype(jnp.bfloat16), "ctx").astype(jnp.float32),
    )
    return (
        y_out,
        x_grad,
        summed_grads[0],
        summed_grads[1],
        summed_grads[2],
        summed_grads[3],
        summed_grads[4],
        summed_grads[5],
        summed_grads[6],
        summed_grads[7],
        summed_grads[8],
    )


def solution(mesh):
    placed = (
        P("fsdp", "ctx", None),
        P("fsdp", None),
        P("fsdp", None),
        P("fsdp", None),
        P("fsdp", None),
        P("fsdp"),
        P("fsdp", None),
        P("fsdp", None),
        P("fsdp", None),
        P("fsdp"),
        P(),
        P("fsdp", "ctx", None),
    )
    return jax.shard_map(
        local,
        mesh=mesh,
        in_specs=placed,
        out_specs=(
            P("fsdp", "ctx", None),
            P("fsdp", "ctx", None),
            P("fsdp", None),
            P("fsdp", None),
            P("fsdp", None),
            P("fsdp", None),
            P("fsdp"),
            P("fsdp", None),
            P("fsdp", None),
            P("fsdp", None),
            P("fsdp"),
        ),
        check_vma=False,
    )
```

profile of v0, /device:TPU:0, one launch (start us, length us, event | category | flops | bytes accessed | tf_op | source)
XLA Modules:
  0.0 655.3 jit_solution(17104645423890764450)
XLA Ops:
  18.4 54.9 %all_gather.35 = bf16[2,1024,3,64]{3,0,2,1:T(2,128)(2,1)} all-gather(bf16[2,64,3,64]{3,0,2,1:T(2,128)(2,1)S(1)} %copy.115), channel_id=1, replica_groups=mesh['ctx'=16,'fsdp'=2] {'ctx'}, dimensions={1}, use_global_device_ids=true | all-gather | bytes 835584 | tf_op jit(solution)/shard_map/all_gather | solution.py:149
  84.5 49.6 %all_gather.38 = bf16[2,1024,3,64]{3,0,2,1:T(2,128)(2,1)S(1)} all-gather(bf16[2,64,3,64]{3,0,2,1:T(2,128)(2,1)S(1)} %copy.121), channel_id=1, replica_groups=mesh['ctx'=16,'fsdp'=2] {'ctx'}, dimensions={1}, use_global_device_ids=true | all-gather | bytes 835584 | tf_op jit(solution)/shard_map/all_gather | solution.py:150
  163.3 216.1 %while.25 = (s32[]{:T(128)}, bf16[2,64,3,64]{3,1,2,0:T(8,128)(2,1)S(1)}, bf16[2,64,3,64]{3,1,2,0:T(8,128)(2,1)S(1)}, f32[2,3,3,64,64]{4,3,2,1,0:T(8,128)S(1)}, f...) while((s32[]{:T(128)}, ...), condition=%wide.region_10.11_spmd.clone, body=%wide.region_8.10_spmd.clone.sunk | while | flops 48082768 | bytes 4246918 | solution.py:257
  168.7 8.0 %collective-permute-done.2 = bf16[2,64,3,64]{3,1,2,0:T(8,128)(2,1)S(1)} collective-permute-done((bf16[2,64,3,64]{3,1,2,0:T(8,128)(2,1)S(1)}, bf16[2,64,3,64]{3,1,2,0:T(8,128)(2,1)S(1)}, u32[]{:S(2)}, u32[]{:S(2)}) %collective-permute-start.2) | collective-permute-done | bytes 49184 | tf_op jit(solution)/shard_map/while/body/eval_jaxpr/ppermute | solution.py:17
  182.3 8.6 %collective-permute-done.2 = bf16[2,64,3,64]{3,1,2,0:T(8,128)(2,1)S(1)} collective-permute-done((bf16[2,64,3,64]{3,1,2,0:T(8,128)(2,1)S(1)}, bf16[2,64,3,64]{3,1,2,0:T(8,128)(2,1)S(1)}, u32[]{:S(2)}, u32[]{:S(2)}) %collective-permute-start.2) | collective-permute-done | bytes 49184 | tf_op jit(solution)/shard_map/while/body/eval_jaxpr/ppermute | solution.py:17
  199.3 5.9 collective-permute-done.2
  214.3 5.3 collective-permute-done.2
  228.3 5.3 collective-permute-done.2
  271.3 5.8 collective-permute-done.2
  285.5 6.4 collective-permute-done.2
  301.2 6.1 collective-permute-done.2
  314.8 8.1 %collective-permute-done.2 = bf16[2,64,3,64]{3,1,2,0:T(8,128)(2,1)S(1)} collective-permute-done((bf16[2,64,3,64]{3,1,2,0:T(8,128)(2,1)S(1)}, bf16[2,64,3,64]{3,1,2,0:T(8,128)(2,1)S(1)}, u32[]{:S(2)}, u32[]{:S(2)}) %collective-permute-start.2) | collective-permute-done | bytes 49184 | tf_op jit(solution)/shard_map/while/body/eval_jaxpr/ppermute | solution.py:17
  328.5 8.6 %collective-permute-done.2 = bf16[2,64,3,64]{3,1,2,0:T(8,128)(2,1)S(1)} collective-permute-done((bf16[2,64,3,64]{3,1,2,0:T(8,128)(2,1)S(1)}, bf16[2,64,3,64]{3,1,2,0:T(8,128)(2,1)S(1)}, u32[]{:S(2)}, u32[]{:S(2)}) %collective-permute-start.2) | collective-permute-done | bytes 49184 | tf_op jit(solution)/shard_map/while/body/eval_jaxpr/ppermute | solution.py:17
  344.6 6.6 %collective-permute-done.2 = bf16[2,64,3,64]{3,1,2,0:T(8,128)(2,1)S(1)} collective-permute-done((bf16[2,64,3,64]{3,1,2,0:T(8,128)(2,1)S(1)}, bf16[2,64,3,64]{3,1,2,0:T(8,128)(2,1)S(1)}, u32[]{:S(2)}, u32[]{:S(2)}) %collective-permute-start.2) | collective-permute-done | bytes 49184 | tf_op jit(solution)/shard_map/while/body/eval_jaxpr/ppermute | solution.py:17
  357.6 7.6 %collective-permute-done.2 = bf16[2,64,3,64]{3,1,2,0:T(8,128)(2,1)S(1)} collective-permute-done((bf16[2,64,3,64]{3,1,2,0:T(8,128)(2,1)S(1)}, bf16[2,64,3,64]{3,1,2,0:T(8,128)(2,1)S(1)}, u32[]{:S(2)}, u32[]{:S(2)}) %collective-permute-start.2) | collective-permute-done | bytes 49184 | tf_op jit(solution)/shard_map/while/body/eval_jaxpr/ppermute | solution.py:17
  373.3 5.0 collective-permute-done.2
  381.8 7.3 %collective-permute-done.5 = bf16[2,64,3,64]{1,3,2,0:T(8,128)(2,1)S(1)} collective-permute-done((bf16[2,64,3,64]{1,3,2,0:T(8,128)(2,1)S(1)}, bf16[2,64,3,64]{1,3,2,0:T(8,128)(2,1)S(1)}, u32[]{:S(2)}, u32[]{:S(2)}) %collective-permute-start.5) | collective-permute-done | bytes 49184 | tf_op jit(solution)/shard_map/ppermute | solution.py:17
  405.3 11.5 %reduce-scatter.14.cloned.1.call-done = bf16[288,576]{1,0:T(8,128)(2,1)} async-done(((bf16[576,576]{1,0:T(8,128)(2,1)}), bf16[288,576]{1,0:T(8,128)(2,1)}) %reduce-scatter.14.cloned.1.call-update) | async-done | bytes 331792 | tf_op jit(solution)/shard_map/reduce_scatter | solution.py:320
  416.8 12.2 %reduce-scatter.8.cloned.1.call-done = bf16[288,576]{1,0:T(8,128)(2,1)} async-done(((bf16[576,576]{1,0:T(8,128)(2,1)}), bf16[288,576]{1,0:T(8,128)(2,1)}) %reduce-scatter.8.cloned.1.call-update) | async-done | bytes 331792 | tf_op jit(solution)/shard_map/reduce_scatter | solution.py:311
  429.0 13.3 %reduce-scatter.18.cloned.1.call-done = bf16[288,1536]{1,0:T(8,128)(2,1)} async-done(((bf16[576,1536]{1,0:T(8,128)(2,1)}), bf16[288,1536]{1,0:T(8,128)(2,1)}) %reduce-scatter.18.cloned.1.call-update) | async-done | bytes 884752 | tf_op jit(solution)/shard_map/reduce_scatter | solution.py:329
  442.4 13.4 %reduce-scatter.16.cloned.1.call-done = bf16[288,1536]{1,0:T(8,128)(2,1)} async-done(((bf16[576,1536]{1,0:T(8,128)(2,1)}), bf16[288,1536]{1,0:T(8,128)(2,1)}) %reduce-scatter.16.cloned.1.call-update) | async-done | bytes 884752 | tf_op jit(solution)/shard_map/reduce_scatter | solution.py:326
  455.8 13.2 %reduce-scatter.20.cloned.1.call-done = bf16[768,576]{0,1:T(8,128)(2,1)} async-done(((bf16[1536,576]{0,1:T(8,128)(2,1)}), bf16[768,576]{0,1:T(8,128)(2,1)}) %reduce-scatter.20.cloned.1.call-update) | async-done | bytes 884752 | tf_op jit(solution)/shard_map/reduce_scatter | solution.py:332
  476.4 43.7 %all-reduce.4 = (bf16[288]{0:T(512)(128)(2,1)S(1)}, bf16[288]{0:T(512)(128)(2,1)S(1)}) all-reduce(bf16[288]{0:T(512)(128)(2,1)S(1)} %dynamic-slice.3, bf16[288]{0:T(512)(128)(2,1)S(1)} %dynamic-slice.5), channel_id=1, replica_groups=mesh['ctx'=16,'fsdp'=2] {'ctx'}, use_global_device_ids=true, to_apply=%region_23.24 | all-reduce | flops 576 | bytes 2304 | tf_op jit(solution)/shard_map/psum | solution.py:344
  522.2 117.8 %all-reduce.10.cloned.1.call-done = (bf16[288,576]{1,0:T(8,128)(2,1)}, bf16[288,192]{1,0:T(8,128)(2,1)}, bf16[288,192]{1,0:T(8,128)(2,1)}, bf16[288,576]{1,0:T(8...) async-done(((bf16[288,576]{1,0:T(8,128)(2,1)}, bf16[288,192]{1,0:T(8,128)(2,1)}, bf16[288,192]{1,0:T(8,128)(2,1)}, ...) | async-done | bytes 3538960 | tf_op jit(solution)/shard_map/psum | solution.py:340
  (549 shorter events, 212.7 us)
Async XLA Ops:
  7.2 141.5 %all-gather.4.cloned.1.call-start = ((), (), s32[]{:S(2)}) async-start(), calls=%async_computation.7 | async-start | bytes 2654208 | tf_op jit(solution)/shard_map/all_gather | solution.py:100
  8.0 143.7 %all-gather.6.cloned.1.call-start = ((), (), s32[]{:S(2)}) async-start(), calls=%async_computation.8 | async-start | bytes 2654208 | tf_op jit(solution)/shard_map/all_gather | solution.py:101
  8.7 145.8 %all-gather.8.cloned.1.call-start = ((), (), s32[]{:S(2)}) async-start(), calls=%async_computation.9 | async-start | bytes 2654208 | tf_op jit(solution)/shard_map/all_gather | solution.py:102
  9.4 392.2 %reduce-scatter.12.cloned.1.call-start = ((), (), s32[]{:S(2)}) async-start(), calls=%async_computation.12 | async-start | bytes 442368 | tf_op jit(solution)/shard_map/reduce_scatter | solution.py:317
  163.3 14.8 %collective-permute-start = (bf16[2,64,3,64]{3,1,2,0:T(8,128)(2,1)S(1)}, bf16[2,64,3,64]{3,1,2,0:T(8,128)(2,1)S(1)}, u32[]{:S(2)}, u32[]{:S(2)}) collective-permute-start(bf16[2,64,3,64]{3,1,2,0:T(8,128)(2,1)S(1)} %copy.200), channel_id=1, source_target_pairs={{30,0},{0,2},{2,4},{4,6},{6,8},{8,10},{10,12},{12,14},{14,16},{16,... | collective-permute-start | bytes 147464 | tf_op jit(solution)/shard_map/while/body/eval_jaxpr/ppermute | solution.py:17
  206.5 14.2 %collective-permute-start = (bf16[2,64,3,64]{3,1,2,0:T(8,128)(2,1)S(1)}, bf16[2,64,3,64]{3,1,2,0:T(8,128)(2,1)S(1)}, u32[]{:S(2)}, u32[]{:S(2)}) collective-permute-start(bf16[2,64,3,64]{3,1,2,0:T(8,128)(2,1)S(1)} %copy.200), channel_id=1, source_target_pairs={{30,0},{0,2},{2,4},{4,6},{6,8},{8,10},{10,12},{12,14},{14,16},{16,... | collective-permute-start | bytes 147464 | tf_op jit(solution)/shard_map/while/body/eval_jaxpr/ppermute | solution.py:17
  206.5 14.2 %collective-permute-start.1 = (bf16[2,64,3,64]{3,1,2,0:T(8,128)(2,1)S(1)}, bf16[2,64,3,64]{3,1,2,0:T(8,128)(2,1)S(1)}, u32[]{:S(2)}, u32[]{:S(2)}) collective-permute-start(bf16[2,64,3,64]{3,1,2,0:T(8,128)(2,1)S(1)} %copy.201), channel_id=1, source_target_pairs={{30,0},{0,2},{2,4},{4,6},{6,8},{8,10},{10,12},{12,14},{14,16},{16,... | collective-permute-start | bytes 147464 | tf_op jit(solution)/shard_map/while/body/eval_jaxpr/ppermute | solution.py:17
  248.1 16.2 %collective-permute-start = (bf16[2,64,3,64]{3,1,2,0:T(8,128)(2,1)S(1)}, bf16[2,64,3,64]{3,1,2,0:T(8,128)(2,1)S(1)}, u32[]{:S(2)}, u32[]{:S(2)}) collective-permute-start(bf16[2,64,3,64]{3,1,2,0:T(8,128)(2,1)S(1)} %copy.200), channel_id=1, source_target_pairs={{30,0},{0,2},{2,4},{4,6},{6,8},{8,10},{10,12},{12,14},{14,16},{16,... | collective-permute-start | bytes 147464 | tf_op jit(solution)/shard_map/while/body/eval_jaxpr/ppermute | solution.py:17
  248.3 16.0 %collective-permute-start.1 = (bf16[2,64,3,64]{3,1,2,0:T(8,128)(2,1)S(1)}, bf16[2,64,3,64]{3,1,2,0:T(8,128)(2,1)S(1)}, u32[]{:S(2)}, u32[]{:S(2)}) collective-permute-start(bf16[2,64,3,64]{3,1,2,0:T(8,128)(2,1)S(1)} %copy.201), channel_id=1, source_target_pairs={{30,0},{0,2},{2,4},{4,6},{6,8},{8,10},{10,12},{12,14},{14,16},{16,... | collective-permute-start | bytes 147464 | tf_op jit(solution)/shard_map/while/body/eval_jaxpr/ppermute | solution.py:17
  264.3 14.5 %collective-permute-start = (bf16[2,64,3,64]{3,1,2,0:T(8,128)(2,1)S(1)}, bf16[2,64,3,64]{3,1,2,0:T(8,128)(2,1)S(1)}, u32[]{:S(2)}, u32[]{:S(2)}) collective-permute-start(bf16[2,64,3,64]{3,1,2,0:T(8,128)(2,1)S(1)} %copy.200), channel_id=1, source_target_pairs={{30,0},{0,2},{2,4},{4,6},{6,8},{8,10},{10,12},{12,14},{14,16},{16,... | collective-permute-start | bytes 147464 | tf_op jit(solution)/shard_map/while/body/eval_jaxpr/ppermute | solution.py:17
  264.4 14.4 %collective-permute-start.1 = (bf16[2,64,3,64]{3,1,2,0:T(8,128)(2,1)S(1)}, bf16[2,64,3,64]{3,1,2,0:T(8,128)(2,1)S(1)}, u32[]{:S(2)}, u32[]{:S(2)}) collective-permute-start(bf16[2,64,3,64]{3,1,2,0:T(8,128)(2,1)S(1)} %copy.201), channel_id=1, source_target_pairs={{30,0},{0,2},{2,4},{4,6},{6,8},{8,10},{10,12},{12,14},{14,16},{16,... | collective-permute-start | bytes 147464 | tf_op jit(solution)/shard_map/while/body/eval_jaxpr/ppermute | solution.py:17
  278.9 15.0 %collective-permute-start = (bf16[2,64,3,64]{3,1,2,0:T(8,128)(2,1)S(1)}, bf16[2,64,3,64]{3,1,2,0:T(8,128)(2,1)S(1)}, u32[]{:S(2)}, u32[]{:S(2)}) collective-permute-start(bf16[2,64,3,64]{3,1,2,0:T(8,128)(2,1)S(1)} %copy.200), channel_id=1, source_target_pairs={{30,0},{0,2},{2,4},{4,6},{6,8},{8,10},{10,12},{12,14},{14,16},{16,... | collective-permute-start | bytes 147464 | tf_op jit(solution)/shard_map/while/body/eval_jaxpr/ppermute | solution.py:17
  279.0 15.0 %collective-permute-start.1 = (bf16[2,64,3,64]{3,1,2,0:T(8,128)(2,1)S(1)}, bf16[2,64,3,64]{3,1,2,0:T(8,128)(2,1)S(1)}, u32[]{:S(2)}, u32[]{:S(2)}) collective-permute-start(bf16[2,64,3,64]{3,1,2,0:T(8,128)(2,1)S(1)} %copy.201), channel_id=1, source_target_pairs={{30,0},{0,2},{2,4},{4,6},{6,8},{8,10},{10,12},{12,14},{14,16},{16,... | collective-permute-start | bytes 147464 | tf_op jit(solution)/shard_map/while/body/eval_jaxpr/ppermute | solution.py:17
  294.0 15.4 %collective-permute-start = (bf16[2,64,3,64]{3,1,2,0:T(8,128)(2,1)S(1)}, bf16[2,64,3,64]{3,1,2,0:T(8,128)(2,1)S(1)}, u32[]{:S(2)}, u32[]{:S(2)}) collective-permute-start(bf16[2,64,3,64]{3,1,2,0:T(8,128)(2,1)S(1)} %copy.200), channel_id=1, source_target_pairs={{30,0},{0,2},{2,4},{4,6},{6,8},{8,10},{10,12},{12,14},{14,16},{16,... | collective-permute-start | bytes 147464 | tf_op jit(solution)/shard_map/while/body/eval_jaxpr/ppermute | solution.py:17
  294.1 15.4 %collective-permute-start.1 = (bf16[2,64,3,64]{3,1,2,0:T(8,128)(2,1)S(1)}, bf16[2,64,3,64]{3,1,2,0:T(8,128)(2,1)S(1)}, u32[]{:S(2)}, u32[]{:S(2)}) collective-permute-start(bf16[2,64,3,64]{3,1,2,0:T(8,128)(2,1)S(1)} %copy.201), channel_id=1, source_target_pairs={{30,0},{0,2},{2,4},{4,6},{6,8},{8,10},{10,12},{12,14},{14,16},{16,... | collective-permute-start | bytes 147464 | tf_op jit(solution)/shard_map/while/body/eval_jaxpr/ppermute | solution.py:17
  309.5 14.8 %collective-permute-start = (bf16[2,64,3,64]{3,1,2,0:T(8,128)(2,1)S(1)}, bf16[2,64,3,64]{3,1,2,0:T(8,128)(2,1)S(1)}, u32[]{:S(2)}, u32[]{:S(2)}) collective-permute-start(bf16[2,64,3,64]{3,1,2,0:T(8,128)(2,1)S(1)} %copy.200), channel_id=1, source_target_pairs={{30,0},{0,2},{2,4},{4,6},{6,8},{8,10},{10,12},{12,14},{14,16},{16,... | collective-permute-start | bytes 147464 | tf_op jit(solution)/shard_map/while/body/eval_jaxpr/ppermute | solution.py:17
  309.5 14.7 %collective-permute-start.1 = (bf16[2,64,3,64]{3,1,2,0:T(8,128)(2,1)S(1)}, bf16[2,64,3,64]{3,1,2,0:T(8,128)(2,1)S(1)}, u32[]{:S(2)}, u32[]{:S(2)}) collective-permute-start(bf16[2,64,3,64]{3,1,2,0:T(8,128)(2,1)S(1)} %copy.201), channel_id=1, source_target_pairs={{30,0},{0,2},{2,4},{4,6},{6,8},{8,10},{10,12},{12,14},{14,16},{16,... | collective-permute-start | bytes 147464 | tf_op jit(solution)/shard_map/while/body/eval_jaxpr/ppermute | solution.py:17
  390.3 15.0 %reduce-scatter.10.cloned.1.call-start = ((), (), s32[]{:S(2)}) async-start(), calls=%async_computation.11 | async-start | bytes 442368 | tf_op jit(solution)/shard_map/reduce_scatter | solution.py:314
  391.7 25.1 %reduce-scatter.14.cloned.1.call-start = ((), (), s32[]{:S(2)}) async-start(), calls=%async_computation.13 | async-start | bytes 1105920 | tf_op jit(solution)/shard_map/reduce_scatter | solution.py:320
  393.0 36.0 %reduce-scatter.8.cloned.1.call-start = ((), (), s32[]{:S(2)}) async-start(), calls=%async_computation.10 | async-start | bytes 1105920 | tf_op jit(solution)/shard_map/reduce_scatter | solution.py:311
  395.5 46.8 %reduce-scatter.18.cloned.1.call-start = ((), (), s32[]{:S(2)}) async-start(), calls=%async_computation.15 | async-start | bytes 2654208 | tf_op jit(solution)/shard_map/reduce_scatter | solution.py:329
  397.5 58.3 %reduce-scatter.16.cloned.1.call-start = ((), (), s32[]{:S(2)}) async-start(), calls=%async_computation.14 | async-start | bytes 2654208 | tf_op jit(solution)/shard_map/reduce_scatter | solution.py:326
  399.4 69.6 %reduce-scatter.20.cloned.1.call-start = ((), (), s32[]{:S(2)}) async-start(), calls=%async_computation.16 | async-start | bytes 2654208 | tf_op jit(solution)/shard_map/reduce_scatter | solution.py:332
  401.3 238.7 %all-reduce.10.cloned.1.call-start = ((), (), s32[]{:S(2)}) async-start(), calls=%async_computation.17 | async-start | bytes 7372800 | tf_op jit(solution)/shard_map/psum | solution.py:340
  (100 other events, 1104.2 us)
Sparse Core Ops, SparseCore 0:
  9.6 12.7 all-gather.3
  24.0 11.2 all-gather.5
  36.8 11.2 all-gather.7
  390.5 3.8 reduce-scatter.11
  396.4 8.8 reduce-scatter.9
  407.4 9.3 reduce-scatter.13
  419.6 9.3 reduce-scatter.7
  431.9 10.4 reduce-scatter.17
  445.3 10.4 reduce-scatter.15
  458.5 10.4 reduce-scatter.19
  476.6 163.4 all-reduce.9
where the time goes:
time: 657 us; the launch traced here: 655 us
  waiting for transfers between devices  310 us (47%)
  blocking collectives  162 us (25%)
  matrix products  68.4 us (10%)
  other arithmetic  44.1 us (7%)
  starting transfers between devices  41.7 us (6%)
  between operations  16.2 us (2%)
  local copies, waits for them, and re-layouts  10.6 us (2%)
    ppermute x62, waiting for transfers between devices, shifted(): return lax.ppermute(block, axis, route)  123 us
    psum x1, waiting for transfers between devices, local(): lax.psum(owned_grads[0].astype(jnp.bfloat16), 'ctx').astype(jnp.float32)  118 us
    all_gather x1, blocking collectives, local(): key_part = lax.all_gather(key_rows, 'ctx', axis=1, tiled=True)  54.9 us
    all_gather x1, blocking collectives, local(): value_part = lax.all_gather(value_rows, 'ctx', axis=1, tiled=True)  49.6 us
    psum x1, blocking collectives, local(): lax.psum(owned_grads[4].astype(jnp.bfloat16), 'ctx').astype(jnp.float32)  43.7 us
    ppermute x62, starting transfers between devices, shifted(): return lax.ppermute(block, axis, route)  41 us
    dot_general x16, matrix products, block_grads(): jnp.einsum('sqkgd,snkd->skgqn', queries, key_part, preferred_element_type...  17 us
    reduce_scatter x1, waiting for transfers between devices, local(): lax.psum_scatter(grad_wgate.astype(jnp.bfloat16), 'fsdp', scatter_dimensi...  13.4 us
  transfers between devices with their start and end apart: 73, of which 38 were waited for; matrix products, arithmetic and copies ran while one was open for 16% of the time, Pallas kernels for 0%

commit v1 on v0

--- a/solution.py
+++ b/solution.py
@@ -1,3 +1,4 @@
+import functools
 import jax
 import jax.numpy as jnp
 from jax import lax
@@ -9,6 +10,24 @@
 epsilon = 1e-05
 theta_base = 100000.0
 masked_value = -1e30
+
+
+def link_the_sums_all(xx, mesh_dim, along_dim):
+    b_next, parts_out = (jax.lax.psum(1, mesh_dim), jax.lax.axis_index(mesh_dim))
+    outer, x_next = (xx, 1)
+    while x_next < b_next:
+        found = []
+        for j in range(b_next):
+            found.append((j, j ^ x_next))
+        piece_now = jax.lax.ppermute(outer, mesh_dim, found)
+        work_now = jnp.concatenate([outer, piece_now], along_dim)
+        view_out = jnp.concatenate([piece_now, outer], along_dim)
+        outer = jnp.where(parts_out & x_next == 0, work_now, view_out)
+        x_next = 2 * x_next
+    return outer
+
+
+map_groups_by_axis = functools.partial(link_the_sums_all, mesh_dim="ctx", along_dim=1)
 
 
 def shifted(block, axis, distance):
@@ -146,7 +165,7 @@
     )
     stat_shape = (seq_count, KV_HEADS, group_size, tok_count)
     running_max = jnp.full(stat_shape, masked_value, jnp.float32)
-    key_part = lax.all_gather(key_rows, "ctx", axis=1, tiled=True)
+    key_part = map_groups_by_axis(key_rows)
     value_part = lax.all_gather(value_rows, "ctx", axis=1, tiled=True)
     key_pos = slot_positions(block_of_slot, jnp.int32(0), key_part.shape[1], half_len)
     visible = query_pos[:, None] >= key_pos[None, :]

time: 657 us -> 616 us (0.938)
  blocking collectives: 162 us -> 109 us
  starting transfers between devices: 41.7 us -> 62.7 us
  waiting for transfers between devices: 310 us -> 324 us
  other arithmetic: 44.1 us -> 31.9 us
  matrix products: 68.4 us -> 57 us
    all_gather x1 -> x0, blocking collectives: 54.9 us -> none  [local(): key_part = lax.all_gather(key_rows, 'ctx', axis=1, tiled=True)]
    convert_element_type x15, other arithmetic: 0.22 us -> 13.6 us  [one_hop(): shifted((grad_value + grad_value_part).astype(jnp.bfloat16), 'ctx', 1)]
    ppermute x62, starting transfers between devices: 41 us -> 53.3 us  [shifted(): return lax.ppermute(block, axis, route)]
    dot_general x16, matrix products: 17 us -> 5.74 us  [block_grads(): jnp.einsum('sqkgd,snkd->skgqn', queries, key_part, preferred_element_type...]
    reduce_sum x17, other arithmetic: 12.7 us -> 1.53 us  [slot_positions(): owners = jnp.sum(jnp.where(slot_match, block_of_slot[None, :], 0), axis=1)]
    ppermute x62, waiting for transfers between devices: 123 us -> 133 us  [shifted(): return lax.ppermute(block, axis, route)]
    ge x16, other arithmetic: 12.3 us -> 1.83 us  [block_grads(): visible = query_pos[:, None] >= key_pos[None, :]]
    ppermute x0 -> x4, starting transfers between devices: none -> 8.73 us  [link_the_sums_all(): piece_now = jax.lax.ppermute(outer, mesh_dim, found)]
  transfers between devices with their start and end apart: 73 -> 77, of which waited for: 38 -> 40; matrix products, arithmetic and copies ran while one was open for 16% -> 13% of each run, Pallas kernels for 0% -> 0%
where the time goes in v1:
time: 616 us; the launch traced here: 615 us
  waiting for transfers between devices  324 us (53%)
  blocking collectives  109 us (18%)
  starting transfers between devices  62.7 us (10%)
  matrix products  57 us (9%)
  other arithmetic  31.9 us (5%)
  between operations  16.4 us (3%)
  local copies, waits for them, and re-layouts  10.9 us (2%)
    ppermute x62, waiting for transfers between devices, shifted(): return lax.ppermute(block, axis, route)  133 us
    psum x1, waiting for transfers between devices, local(): lax.psum(owned_grads[0].astype(jnp.bfloat16), 'ctx').astype(jnp.float32)  118 us
    ppermute x62, starting transfers between devices, shifted(): return lax.ppermute(block, axis, route)  53.3 us
    all_gather x1, blocking collectives, local(): value_part = lax.all_gather(value_rows, 'ctx', axis=1, tiled=True)  51.4 us
    psum x1, blocking collectives, local(): lax.psum(owned_grads[4].astype(jnp.bfloat16), 'ctx').astype(jnp.float32)  43.7 us
    convert_element_type x15, other arithmetic, one_hop(): shifted((grad_value + grad_value_part).astype(jnp.bfloat16), 'ctx', 1)  13.6 us
    reduce_scatter x1, waiting for transfers between devices, local(): lax.psum_scatter(grad_wgate.astype(jnp.bfloat16), 'fsdp', scatter_dimensi...  13.4 us
    reduce_scatter x1, waiting for transfers between devices, local(): lax.psum_scatter(grad_wup.astype(jnp.bfloat16), 'fsdp', scatter_dimension...  13.3 us
  transfers between devices with their start and end apart: 77, of which 40 were waited for; matrix products, arithmetic and copies ran while one was open for 13% of the time, Pallas kernels for 0%

profile of v1, /device:TPU:0, one launch (start us, length us, event | category | flops | bytes accessed | tf_op | source)
XLA Modules:
  0.0 614.8 jit_solution(11398062615757228413)
XLA Ops:
  43.0 51.4 %all_gather.34 = bf16[2,1024,3,64]{3,0,2,1:T(2,128)(2,1)S(1)} all-gather(bf16[2,64,3,64]{3,0,2,1:T(2,128)(2,1)S(1)} %copy.115), channel_id=1, replica_groups=mesh['ctx'=16,'fsdp'=2] {'ctx'}, dimensions={1}, use_global_device_ids=true | all-gather | bytes 835584 | tf_op jit(solution)/shard_map/all_gather | solution.py:169
  116.3 221.8 %while.25 = (s32[]{:T(128)}, bf16[2,64,3,64]{3,1,2,0:T(8,128)(2,1)S(1)}, bf16[2,64,3,64]{3,1,2,0:T(8,128)(2,1)S(1)}, f32[2,3,3,64,64]{4,3,2,1,0:T(8,128)S(1)}, f...) while((s32[]{:T(128)}, ...), condition=%wide.region_10.11_spmd.clone, body=%wide.region_8.10_spmd.clone.sunk | while | flops 48082768 | bytes 4246918 | solution.py:276
  126.0 4.3 collective-permute-start.3
  157.3 5.4 collective-permute-done.2
  171.9 6.6 %collective-permute-done.2 = bf16[2,64,3,64]{3,1,2,0:T(8,128)(2,1)S(1)} collective-permute-done((bf16[2,64,3,64]{3,1,2,0:T(8,128)(2,1)S(1)}, bf16[2,64,3,64]{3,1,2,0:T(8,128)(2,1)S(1)}, u32[]{:S(2)}, u32[]{:S(2)}) %collective-permute-start.2) | collective-permute-done | bytes 49184 | tf_op jit(solution)/shard_map/while/body/eval_jaxpr/ppermute | solution.py:36
  186.0 9.2 %collective-permute-done.2 = bf16[2,64,3,64]{3,1,2,0:T(8,128)(2,1)S(1)} collective-permute-done((bf16[2,64,3,64]{3,1,2,0:T(8,128)(2,1)S(1)}, bf16[2,64,3,64]{3,1,2,0:T(8,128)(2,1)S(1)}, u32[]{:S(2)}, u32[]{:S(2)}) %collective-permute-start.2) | collective-permute-done | bytes 49184 | tf_op jit(solution)/shard_map/while/body/eval_jaxpr/ppermute | solution.py:36
  200.3 11.3 %collective-permute-done.2 = bf16[2,64,3,64]{3,1,2,0:T(8,128)(2,1)S(1)} collective-permute-done((bf16[2,64,3,64]{3,1,2,0:T(8,128)(2,1)S(1)}, bf16[2,64,3,64]{3,1,2,0:T(8,128)(2,1)S(1)}, u32[]{:S(2)}, u32[]{:S(2)}) %collective-permute-start.2) | collective-permute-done | bytes 49184 | tf_op jit(solution)/shard_map/while/body/eval_jaxpr/ppermute | solution.py:36
  216.0 10.4 %collective-permute-done.2 = bf16[2,64,3,64]{3,1,2,0:T(8,128)(2,1)S(1)} collective-permute-done((bf16[2,64,3,64]{3,1,2,0:T(8,128)(2,1)S(1)}, bf16[2,64,3,64]{3,1,2,0:T(8,128)(2,1)S(1)}, u32[]{:S(2)}, u32[]{:S(2)}) %collective-permute-start.2) | collective-permute-done | bytes 49184 | tf_op jit(solution)/shard_map/while/body/eval_jaxpr/ppermute | solution.py:36
  230.6 9.3 %collective-permute-done.2 = bf16[2,64,3,64]{3,1,2,0:T(8,128)(2,1)S(1)} collective-permute-done((bf16[2,64,3,64]{3,1,2,0:T(8,128)(2,1)S(1)}, bf16[2,64,3,64]{3,1,2,0:T(8,128)(2,1)S(1)}, u32[]{:S(2)}, u32[]{:S(2)}) %collective-permute-start.2) | collective-permute-done | bytes 49184 | tf_op jit(solution)/shard_map/while/body/eval_jaxpr/ppermute | solution.py:36
  244.3 8.3 %collective-permute-done.2 = bf16[2,64,3,64]{3,1,2,0:T(8,128)(2,1)S(1)} collective-permute-done((bf16[2,64,3,64]{3,1,2,0:T(8,128)(2,1)S(1)}, bf16[2,64,3,64]{3,1,2,0:T(8,128)(2,1)S(1)}, u32[]{:S(2)}, u32[]{:S(2)}) %collective-permute-start.2) | collective-permute-done | bytes 49184 | tf_op jit(solution)/shard_map/while/body/eval_jaxpr/ppermute | solution.py:36
  256.9 8.2 %collective-permute-done.2 = bf16[2,64,3,64]{3,1,2,0:T(8,128)(2,1)S(1)} collective-permute-done((bf16[2,64,3,64]{3,1,2,0:T(8,128)(2,1)S(1)}, bf16[2,64,3,64]{3,1,2,0:T(8,128)(2,1)S(1)}, u32[]{:S(2)}, u32[]{:S(2)}) %collective-permute-start.2) | collective-permute-done | bytes 49184 | tf_op jit(solution)/shard_map/while/body/eval_jaxpr/ppermute | solution.py:36
  272.1 5.4 collective-permute-done.2
  303.2 4.6 collective-permute-done.2
  312.8 4.1 collective-permute-start.3
  317.3 6.2 %collective-permute-done.2 = bf16[2,64,3,64]{3,1,2,0:T(8,128)(2,1)S(1)} collective-permute-done((bf16[2,64,3,64]{3,1,2,0:T(8,128)(2,1)S(1)}, bf16[2,64,3,64]{3,1,2,0:T(8,128)(2,1)S(1)}, u32[]{:S(2)}, u32[]{:S(2)}) %collective-permute-start.2) | collective-permute-done | bytes 49184 | tf_op jit(solution)/shard_map/while/body/eval_jaxpr/ppermute | solution.py:36
  330.0 6.0 collective-permute-done.2
  340.2 7.8 %collective-permute-done.9 = bf16[2,64,3,64]{1,3,2,0:T(8,128)(2,1)} collective-permute-done((bf16[2,64,3,64]{1,3,2,0:T(8,128)(2,1)}, bf16[2,64,3,64]{1,3,2,0:T(8,128)(2,1)}, u32[]{:S(2)}, u32[]{:S(2)}) %collective-permute-start.9) | collective-permute-done | bytes 49184 | tf_op jit(solution)/shard_map/ppermute | solution.py:36
  364.8 11.5 %reduce-scatter.14.cloned.1.call-done = bf16[288,576]{1,0:T(8,128)(2,1)} async-done(((bf16[576,576]{1,0:T(8,128)(2,1)}), bf16[288,576]{1,0:T(8,128)(2,1)}) %reduce-scatter.14.cloned.1.call-update) | async-done | bytes 331792 | tf_op jit(solution)/shard_map/reduce_scatter | solution.py:339
  376.3 12.2 %reduce-scatter.8.cloned.1.call-done = bf16[288,576]{1,0:T(8,128)(2,1)} async-done(((bf16[576,576]{1,0:T(8,128)(2,1)}), bf16[288,576]{1,0:T(8,128)(2,1)}) %reduce-scatter.8.cloned.1.call-update) | async-done | bytes 331792 | tf_op jit(solution)/shard_map/reduce_scatter | solution.py:330
  388.5 13.3 %reduce-scatter.18.cloned.1.call-done = bf16[288,1536]{1,0:T(8,128)(2,1)} async-done(((bf16[576,1536]{1,0:T(8,128)(2,1)}), bf16[288,1536]{1,0:T(8,128)(2,1)}) %reduce-scatter.18.cloned.1.call-update) | async-done | bytes 884752 | tf_op jit(solution)/shard_map/reduce_scatter | solution.py:348
  401.8 13.4 %reduce-scatter.16.cloned.1.call-done = bf16[288,1536]{1,0:T(8,128)(2,1)} async-done(((bf16[576,1536]{1,0:T(8,128)(2,1)}), bf16[288,1536]{1,0:T(8,128)(2,1)}) %reduce-scatter.16.cloned.1.call-update) | async-done | bytes 884752 | tf_op jit(solution)/shard_map/reduce_scatter | solution.py:345
  415.3 13.2 %reduce-scatter.20.cloned.1.call-done = bf16[768,576]{0,1:T(8,128)(2,1)} async-done(((bf16[1536,576]{0,1:T(8,128)(2,1)}), bf16[768,576]{0,1:T(8,128)(2,1)}) %reduce-scatter.20.cloned.1.call-update) | async-done | bytes 884752 | tf_op jit(solution)/shard_map/reduce_scatter | solution.py:351
  435.9 43.7 %all-reduce.4 = (bf16[288]{0:T(512)(128)(2,1)S(1)}, bf16[288]{0:T(512)(128)(2,1)S(1)}) all-reduce(bf16[288]{0:T(512)(128)(2,1)S(1)} %dynamic-slice.3, bf16[288]{0:T(512)(128)(2,1)S(1)} %dynamic-slice.5), channel_id=1, replica_groups=mesh['ctx'=16,'fsdp'=2] {'ctx'}, use_global_device_ids=true, to_apply=%region_23.24 | all-reduce | flops 576 | bytes 2304 | tf_op jit(solution)/shard_map/psum | solution.py:363
  481.7 117.8 %all-reduce.10.cloned.1.call-done = (bf16[288,576]{1,0:T(8,128)(2,1)}, bf16[288,192]{1,0:T(8,128)(2,1)}, bf16[288,192]{1,0:T(8,128)(2,1)}, bf16[288,576]{1,0:T(8...) async-done(((bf16[288,576]{1,0:T(8,128)(2,1)}, bf16[288,192]{1,0:T(8,128)(2,1)}, bf16[288,192]{1,0:T(8,128)(2,1)}, ...) | async-done | bytes 3538960 | tf_op jit(solution)/shard_map/psum | solution.py:359
  (576 shorter events, 212.6 us)
Async XLA Ops:
  7.2 94.4 %all-gather.4.cloned.1.call-start = ((), (), s32[]{:S(2)}) async-start(), calls=%async_computation.7 | async-start | bytes 2654208 | tf_op jit(solution)/shard_map/all_gather | solution.py:119
  8.0 96.6 %all-gather.6.cloned.1.call-start = ((), (), s32[]{:S(2)}) async-start(), calls=%async_computation.8 | async-start | bytes 2654208 | tf_op jit(solution)/shard_map/all_gather | solution.py:120
  8.7 98.7 %all-gather.8.cloned.1.call-start = ((), (), s32[]{:S(2)}) async-start(), calls=%async_computation.9 | async-start | bytes 2654208 | tf_op jit(solution)/shard_map/all_gather | solution.py:121
  19.6 341.9 %reduce-scatter.12.cloned.1.call-start = ((), (), s32[]{:S(2)}) async-start(), calls=%async_computation.12 | async-start | bytes 442368 | tf_op jit(solution)/shard_map/reduce_scatter | solution.py:336
  38.3 56.1 %collective-permute-start.7 = (bf16[2,512,3,64]{1,3,2,0:T(8,128)(2,1)S(1)}, bf16[2,512,3,64]{1,3,2,0:T(8,128)(2,1)}, u32[]{:S(2)}, u32[]{:S(2)}) collective-permute-start(bf16[2,512,3,64]{1,3,2,0:T(8,128)(2,1)S(1)} %maximum_select_fusion.1), channel_id=1, source_target_pairs={{0,16},{2,18},{4,20},{6,22},{8,24},{10,26},{12,28},{14,30},{16,0},... | collective-permute-start | bytes 1179656 | tf_op jit(solution)/shard_map/ppermute | solution.py:22
  116.3 19.6 %collective-permute-start = (bf16[2,64,3,64]{3,1,2,0:T(8,128)(2,1)S(1)}, bf16[2,64,3,64]{3,1,2,0:T(8,128)(2,1)S(1)}, u32[]{:S(2)}, u32[]{:S(2)}) collective-permute-start(bf16[2,64,3,64]{3,1,2,0:T(8,128)(2,1)S(1)} %copy.188), channel_id=1, source_target_pairs={{30,0},{0,2},{2,4},{4,6},{6,8},{8,10},{10,12},{12,14},{14,16},{16,... | collective-permute-start | bytes 147464 | tf_op jit(solution)/shard_map/while/body/eval_jaxpr/ppermute | solution.py:36
  119.9 16.0 %collective-permute-start.1 = (bf16[2,64,3,64]{3,1,2,0:T(8,128)(2,1)S(1)}, bf16[2,64,3,64]{3,1,2,0:T(8,128)(2,1)S(1)}, u32[]{:S(2)}, u32[]{:S(2)}) collective-permute-start(bf16[2,64,3,64]{3,1,2,0:T(8,128)(2,1)S(1)} %copy.189), channel_id=1, source_target_pairs={{30,0},{0,2},{2,4},{4,6},{6,8},{8,10},{10,12},{12,14},{14,16},{16,... | collective-permute-start | bytes 147464 | tf_op jit(solution)/shard_map/while/body/eval_jaxpr/ppermute | solution.py:36
  136.0 15.3 %collective-permute-start = (bf16[2,64,3,64]{3,1,2,0:T(8,128)(2,1)S(1)}, bf16[2,64,3,64]{3,1,2,0:T(8,128)(2,1)S(1)}, u32[]{:S(2)}, u32[]{:S(2)}) collective-permute-start(bf16[2,64,3,64]{3,1,2,0:T(8,128)(2,1)S(1)} %copy.188), channel_id=1, source_target_pairs={{30,0},{0,2},{2,4},{4,6},{6,8},{8,10},{10,12},{12,14},{14,16},{16,... | collective-permute-start | bytes 147464 | tf_op jit(solution)/shard_map/while/body/eval_jaxpr/ppermute | solution.py:36
  136.6 14.7 %collective-permute-start.1 = (bf16[2,64,3,64]{3,1,2,0:T(8,128)(2,1)S(1)}, bf16[2,64,3,64]{3,1,2,0:T(8,128)(2,1)S(1)}, u32[]{:S(2)}, u32[]{:S(2)}) collective-permute-start(bf16[2,64,3,64]{3,1,2,0:T(8,128)(2,1)S(1)} %copy.189), channel_id=1, source_target_pairs={{30,0},{0,2},{2,4},{4,6},{6,8},{8,10},{10,12},{12,14},{14,16},{16,... | collective-permute-start | bytes 147464 | tf_op jit(solution)/shard_map/while/body/eval_jaxpr/ppermute | solution.py:36
  165.9 15.7 %collective-permute-start = (bf16[2,64,3,64]{3,1,2,0:T(8,128)(2,1)S(1)}, bf16[2,64,3,64]{3,1,2,0:T(8,128)(2,1)S(1)}, u32[]{:S(2)}, u32[]{:S(2)}) collective-permute-start(bf16[2,64,3,64]{3,1,2,0:T(8,128)(2,1)S(1)} %copy.188), channel_id=1, source_target_pairs={{30,0},{0,2},{2,4},{4,6},{6,8},{8,10},{10,12},{12,14},{14,16},{16,... | collective-permute-start | bytes 147464 | tf_op jit(solution)/shard_map/while/body/eval_jaxpr/ppermute | solution.py:36
  166.0 15.7 %collective-permute-start.1 = (bf16[2,64,3,64]{3,1,2,0:T(8,128)(2,1)S(1)}, bf16[2,64,3,64]{3,1,2,0:T(8,128)(2,1)S(1)}, u32[]{:S(2)}, u32[]{:S(2)}) collective-permute-start(bf16[2,64,3,64]{3,1,2,0:T(8,128)(2,1)S(1)} %copy.189), channel_id=1, source_target_pairs={{30,0},{0,2},{2,4},{4,6},{6,8},{8,10},{10,12},{12,14},{14,16},{16,... | collective-permute-start | bytes 147464 | tf_op jit(solution)/shard_map/while/body/eval_jaxpr/ppermute | solution.py:36
  181.7 16.4 %collective-permute-start = (bf16[2,64,3,64]{3,1,2,0:T(8,128)(2,1)S(1)}, bf16[2,64,3,64]{3,1,2,0:T(8,128)(2,1)S(1)}, u32[]{:S(2)}, u32[]{:S(2)}) collective-permute-start(bf16[2,64,3,64]{3,1,2,0:T(8,128)(2,1)S(1)} %copy.188), channel_id=1, source_target_pairs={{30,0},{0,2},{2,4},{4,6},{6,8},{8,10},{10,12},{12,14},{14,16},{16,... | collective-permute-start | bytes 147464 | tf_op jit(solution)/shard_map/while/body/eval_jaxpr/ppermute | solution.py:36
  181.8 16.4 %collective-permute-start.1 = (bf16[2,64,3,64]{3,1,2,0:T(8,128)(2,1)S(1)}, bf16[2,64,3,64]{3,1,2,0:T(8,128)(2,1)S(1)}, u32[]{:S(2)}, u32[]{:S(2)}) collective-permute-start(bf16[2,64,3,64]{3,1,2,0:T(8,128)(2,1)S(1)} %copy.189), channel_id=1, source_target_pairs={{30,0},{0,2},{2,4},{4,6},{6,8},{8,10},{10,12},{12,14},{14,16},{16,... | collective-permute-start | bytes 147464 | tf_op jit(solution)/shard_map/while/body/eval_jaxpr/ppermute | solution.py:36
  198.2 15.6 %collective-permute-start = (bf16[2,64,3,64]{3,1,2,0:T(8,128)(2,1)S(1)}, bf16[2,64,3,64]{3,1,2,0:T(8,128)(2,1)S(1)}, u32[]{:S(2)}, u32[]{:S(2)}) collective-permute-start(bf16[2,64,3,64]{3,1,2,0:T(8,128)(2,1)S(1)} %copy.188), channel_id=1, source_target_pairs={{30,0},{0,2},{2,4},{4,6},{6,8},{8,10},{10,12},{12,14},{14,16},{16,... | collective-permute-start | bytes 147464 | tf_op jit(solution)/shard_map/while/body/eval_jaxpr/ppermute | solution.py:36
  198.3 15.5 %collective-permute-start.1 = (bf16[2,64,3,64]{3,1,2,0:T(8,128)(2,1)S(1)}, bf16[2,64,3,64]{3,1,2,0:T(8,128)(2,1)S(1)}, u32[]{:S(2)}, u32[]{:S(2)}) collective-permute-start(bf16[2,64,3,64]{3,1,2,0:T(8,128)(2,1)S(1)} %copy.189), channel_id=1, source_target_pairs={{30,0},{0,2},{2,4},{4,6},{6,8},{8,10},{10,12},{12,14},{14,16},{16,... | collective-permute-start | bytes 147464 | tf_op jit(solution)/shard_map/while/body/eval_jaxpr/ppermute | solution.py:36
  294.3 16.6 %collective-permute-start = (bf16[2,64,3,64]{3,1,2,0:T(8,128)(2,1)S(1)}, bf16[2,64,3,64]{3,1,2,0:T(8,128)(2,1)S(1)}, u32[]{:S(2)}, u32[]{:S(2)}) collective-permute-start(bf16[2,64,3,64]{3,1,2,0:T(8,128)(2,1)S(1)} %copy.188), channel_id=1, source_target_pairs={{30,0},{0,2},{2,4},{4,6},{6,8},{8,10},{10,12},{12,14},{14,16},{16,... | collective-permute-start | bytes 147464 | tf_op jit(solution)/shard_map/while/body/eval_jaxpr/ppermute | solution.py:36
  294.4 16.6 %collective-permute-start.1 = (bf16[2,64,3,64]{3,1,2,0:T(8,128)(2,1)S(1)}, bf16[2,64,3,64]{3,1,2,0:T(8,128)(2,1)S(1)}, u32[]{:S(2)}, u32[]{:S(2)}) collective-permute-start(bf16[2,64,3,64]{3,1,2,0:T(8,128)(2,1)S(1)} %copy.189), channel_id=1, source_target_pairs={{30,0},{0,2},{2,4},{4,6},{6,8},{8,10},{10,12},{12,14},{14,16},{16,... | collective-permute-start | bytes 147464 | tf_op jit(solution)/shard_map/while/body/eval_jaxpr/ppermute | solution.py:36
  350.1 14.7 %reduce-scatter.10.cloned.1.call-start = ((), (), s32[]{:S(2)}) async-start(), calls=%async_computation.11 | async-start | bytes 442368 | tf_op jit(solution)/shard_map/reduce_scatter | solution.py:333
  351.5 24.7 %reduce-scatter.14.cloned.1.call-start = ((), (), s32[]{:S(2)}) async-start(), calls=%async_computation.13 | async-start | bytes 1105920 | tf_op jit(solution)/shard_map/reduce_scatter | solution.py:339
  353.1 35.4 %reduce-scatter.8.cloned.1.call-start = ((), (), s32[]{:S(2)}) async-start(), calls=%async_computation.10 | async-start | bytes 1105920 | tf_op jit(solution)/shard_map/reduce_scatter | solution.py:330
  355.6 46.2 %reduce-scatter.18.cloned.1.call-start = ((), (), s32[]{:S(2)}) async-start(), calls=%async_computation.15 | async-start | bytes 2654208 | tf_op jit(solution)/shard_map/reduce_scatter | solution.py:348
  357.5 57.7 %reduce-scatter.16.cloned.1.call-start = ((), (), s32[]{:S(2)}) async-start(), calls=%async_computation.14 | async-start | bytes 2654208 | tf_op jit(solution)/shard_map/reduce_scatter | solution.py:345
  359.4 69.0 %reduce-scatter.20.cloned.1.call-start = ((), (), s32[]{:S(2)}) async-start(), calls=%async_computation.16 | async-start | bytes 2654208 | tf_op jit(solution)/shard_map/reduce_scatter | solution.py:351
  361.4 238.1 %all-reduce.10.cloned.1.call-start = ((), (), s32[]{:S(2)}) async-start(), calls=%async_computation.17 | async-start | bytes 7372800 | tf_op jit(solution)/shard_map/psum | solution.py:359
  (113 other events, 1141.1 us)
Sparse Core Ops, SparseCore 0:
  9.6 13.3 all-gather.3
  24.5 10.8 all-gather.5
  37.0 11.2 all-gather.7
  350.2 3.5 reduce-scatter.11
  355.9 8.8 reduce-scatter.9
  366.9 9.3 reduce-scatter.13
  379.1 9.3 reduce-scatter.7
  391.3 10.4 reduce-scatter.17
  404.8 10.4 reduce-scatter.15
  417.9 10.4 reduce-scatter.19
  436.0 163.4 all-reduce.9
